TPU v7x, 128 devices: a whole 4x4x4 slice. The times are simulated.
128 devices in a mesh: rep: 4 (over z), ten: 32 (over x, y, core).
Axes of the slice: x: 4, y: 4, z: 4, core: 2. Of those that a mesh axis runs over, the one named last changes fastest.
Arguments:
- blocks: bfloat16 [64, 512, 4096], P(None, 'ten'), may hold values from -0.5 to 0.5
- col_counts: int32 [32], replicated, may hold values from 1 to 4, 64 in all
- block_sizes: int32 [32], replicated, may hold values from 32 to 64
- occ_coeff: bfloat16 [2048, 256], P(None, 'rep'), may hold values from -1.5 to 1.5
- occ_weight: float32 [256], P('rep'), may hold values from 0.1 to 1
- virt_green: bfloat16 [2048, 2048], replicated, may hold values from -0.125 to 0.125
Outputs:
- chi: float32 [512, 512], P('ten')
Inputs may be any that keep to these rules, and one draw needn't show every extreme that they name: `col_counts`: each block column holds 1 to 4 nonzero blocks, 64 in all, and some column holds exactly 4.
All inputs are finite; a program needn't handle non-finite values.
Results may differ from a plain program's by a relative error of at most 0.0047.
Values may be sent and summed in bfloat16 or wider, within the bound.
No kernel may reach another device: no remote copies, remote signals or barrier semaphores. Data moves between devices by JAX's collectives and lax.ppermute only.
A program may use at most 192 MiB of HBM per device.

v0:
```python
import functools

import jax
import jax.numpy as jnp
from jax import lax
from jax.experimental import pallas as pl
from jax.experimental.pallas import tpu as pltpu
from jax.sharding import PartitionSpec as P

BS = 64
MOST = 4
LANES = 128
MIB = 1024 * 1024


def half_kernel(counts_ref, sizes_ref, occ_ref, blocks_ref, out_ref, slots, turned, starts):
    block_count = counts_ref.shape[0]
    aux_rows = blocks_ref.shape[1]
    occ_count = BS
    half_x = BS // 2

    def count_up(b, total):
        starts[b] = total
        return total + counts_ref[b]

    lax.fori_loop(0, block_count, count_up, jnp.int32(0))
    slots[...] = jnp.zeros_like(slots)

    x_of = 2 * lax.broadcasted_iota(jnp.int32, (half_x, LANES), 0) + (
        lax.broadcasted_iota(jnp.int32, (half_x, LANES), 1) // BS
    )
    lane = lax.broadcasted_iota(jnp.int32, (BS, LANES), 1)
    low = lane < BS

    def column_pair(m, carry):
        weights = []
        for side in range(2):
            b = 2 * m + side
            first, count = starts[b], counts_ref[b]
            rows = []
            for j in range(MOST):
                offset = (j + 1) // 2 if j % 2 == 1 else -(j // 2)
                row = lax.rem(b + offset + block_count, block_count)
                size = jnp.where(j < count, sizes_ref[row], 0)
                coeff = occ_ref[pl.ds(row * half_x, half_x), :]
                rows.append(jnp.where(x_of < size, coeff, 0.0))

                @pl.when(j < count)
                def _(side=side, j=j, first=first):
                    for t in range(half_x):
                        piece = blocks_ref[first + j, :, t * LANES : (t + 1) * LANES]
                        slots[side, j, pl.ds(t, aux_rows, stride=half_x), :] = piece.astype(jnp.float32)

            weights.append(jnp.transpose(jnp.concatenate(rows, axis=0)).astype(jnp.bfloat16))
        keep = lane < jnp.where(low, sizes_ref[2 * m], sizes_ref[2 * m + 1] + BS)
        for pp in range(aux_rows // 2):
            sums = []
            for side in range(2):
                cols = [
                    jnp.concatenate(
                        [slots[side, j, p * half_x : (p + 1) * half_x, :] for j in range(MOST)], axis=0
                    ).astype(jnp.bfloat16)
                    for p in (2 * pp, 2 * pp + 1)
                ]
                sums.append(
                    jnp.dot(weights[side], jnp.concatenate(cols, axis=1), preferred_element_type=jnp.float32)
                )
            for q in range(2):
                even0 = sums[0][:BS, q * LANES : (q + 1) * LANES]
                odd0 = sums[0][BS:, q * LANES : (q + 1) * LANES]
                even1 = sums[1][:BS, q * LANES : (q + 1) * LANES]
                odd1 = sums[1][BS:, q * LANES : (q + 1) * LANES]
                total = jnp.where(low, even0, odd1) + pltpu.roll(jnp.where(low, even1, odd0), BS, 1)
                turned[pl.ds(2 * pp + q, occ_count, stride=aux_rows), :] = jnp.where(keep, total, 0.0)
        out_ref[:, pl.ds(pl.multiple_of(m * LANES, LANES), LANES)] = turned[...].astype(jnp.bfloat16)
        return carry

    lax.fori_loop(0, block_count // 2, column_pair, 0)


def half_transform(blocks, col_counts, block_sizes, occ_coeff):
    pair_count, aux_rows, _ = blocks.shape
    block_count = col_counts.shape[0]
    occ_count = occ_coeff.shape[1]
    occ = occ_coeff.astype(jnp.float32).reshape(block_count * BS // 2, 2 * occ_count)
    smem = pl.BlockSpec(memory_space=pltpu.SMEM)
    vmem = pl.BlockSpec(memory_space=pltpu.VMEM)
    return pl.pallas_call(
        half_kernel,
        out_shape=jax.ShapeDtypeStruct((occ_count * aux_rows, block_count * BS), jnp.bfloat16),
        in_specs=[smem, smem, vmem, vmem],
        out_specs=vmem,
        scratch_shapes=[
            pltpu.VMEM((2, MOST, aux_rows * BS // 2, LANES), jnp.float32),
            pltpu.VMEM((occ_count * aux_rows, LANES), jnp.float32),
            pltpu.SMEM((block_count,), jnp.int32),
        ],
        compiler_params=pltpu.CompilerParams(vmem_limit_bytes=40 * MIB),
        name="half_transform",
    )(col_counts, block_sizes, occ, blocks)


def response_kernel(weight_ref, half_ref, green_ref, chi_ref, folded, total):
    step = pl.program_id(0)
    sources, own, aux_rows, basis_count = half_ref.shape
    rows = sources * aux_rows
    tile = green_ref.shape[1]

    @pl.when(step == 0)
    def _():
        total[...] = jnp.zeros_like(total)
        for ii in range(own):
            folded[ii] = (
                half_ref[:, ii].astype(jnp.float32).reshape(rows, basis_count) * weight_ref[ii]
            ).astype(jnp.bfloat16)

    columns = pl.ds(pl.multiple_of(step * tile, tile), tile)
    for ii in range(own):
        dressed = jnp.dot(folded[ii], green_ref[...], preferred_element_type=jnp.float32).astype(jnp.bfloat16)
        left = half_ref[:, ii, :, columns].reshape(rows, tile)
        total[...] += lax.dot_general(left, dressed, (((1,), (1,)), ((), ())), preferred_element_type=jnp.float32)

    @pl.when(step == pl.num_programs(0) - 1)
    def _():
        chi_ref[...] = total[...].astype(chi_ref.dtype)


def response(half, weight, virt_green, tile=256):
    sources, own, aux_rows, basis_count = half.shape
    rows = sources * aux_rows
    return pl.pallas_call(
        response_kernel,
        grid=(basis_count // tile,),
        out_shape=jax.ShapeDtypeStruct((rows, rows), jnp.bfloat16),
        in_specs=[
            pl.BlockSpec(memory_space=pltpu.SMEM),
            pl.BlockSpec((sources, own, aux_rows, basis_count), lambda n: (0, 0, 0, 0)),
            pl.BlockSpec((basis_count, tile), lambda n: (0, n)),
        ],
        out_specs=pl.BlockSpec((rows, rows), lambda n: (0, 0)),
        scratch_shapes=[
            pltpu.VMEM((own, rows, basis_count), jnp.bfloat16),
            pltpu.VMEM((rows, rows), jnp.float32),
        ],
        compiler_params=pltpu.CompilerParams(vmem_limit_bytes=40 * MIB),
        name="response",
    )(weight, half, virt_green)


def per_device(blocks, col_counts, block_sizes, occ_coeff, occ_weight, virt_green):
    devices = lax.axis_size("ten")
    _, aux_rows, _ = blocks.shape
    occ_count = occ_coeff.shape[1]
    own = occ_count // devices
    basis_count = devices * BS
    half = half_transform(blocks, col_counts, block_sizes, occ_coeff)
    half = half.reshape(devices, own, aux_rows, basis_count)
    got = lax.all_to_all(half, "ten", split_axis=0, concat_axis=0, tiled=True)
    weight = lax.dynamic_slice(occ_weight, (lax.axis_index("ten") * own,), (own,))
    terms = response(got, weight, virt_green).reshape(devices, aux_rows, devices * aux_rows)
    terms = lax.all_to_all(terms, "ten", split_axis=0, concat_axis=0, tiled=True)
    share = jnp.sum(terms.astype(jnp.float32), axis=0)
    return lax.psum(share, "rep")


def solution(mesh):
    return jax.shard_map(
        per_device,
        mesh=mesh,
        in_specs=(P(None, "ten", None), P(), P(), P(None, "rep"), P("rep"), P()),
        out_specs=P("ten", None),
        check_vma=False,
    )
```

profile of v0, /device:TPU:1, one launch (start us, length us, event | category | flops | bytes accessed | tf_op | source)
XLA Modules:
  0.0 147.5 jit_solution(11279535256415474635)
XLA Ops:
  0.0 1.2 copy.8
  1.2 0.2 reshape.16.occ_ref
  1.4 0.0 copy-start.2
  1.4 3.4 %copy-done.2 = bf16[64,16,4096]{2,1,0:T(8,128)(2,1)S(1)} copy-done((bf16[64,16,4096]{2,1,0:T(8,128)(2,1)S(1)}, bf16[64,16,4096]{2,1,0:T(8,128)(2,1)}, u32[]{:S(2)}) %copy-start.2) | copy-done | bytes 8388632
  4.8 0.0 copy-start.3
  4.8 0.7 copy-done.3
  5.4 0.0 copy-start.4
  5.4 0.7 copy-done.4
  6.1 0.0 copy-start.5
  6.1 24.4 %half_transform.1 = bf16[1024,2048]{1,0:T(8,128)(2,1)S(1)} custom-call(s32[32]{0:T(128)S(1)} %copy-done.3, s32[32]{0:T(128)S(1)} %copy-done.4, f32[1024,128]{1,0:T(8,128)S(1)} %reshape.16.occ_ref, bf16[64,16,4096]{2,1,0:T(8,128)(2,1)S(1)} %copy-done.2), custom_call_target="tpu_custom_call" | custom-call | tf_op jit(solution)/shard_map/half_transform/pallas_call | solution.py:88
  30.5 0.0 copy-start
  30.5 2.0 %copy-done = bf16[1024,2048]{1,0:T(8,128)(2,1)} copy-done((bf16[1024,2048]{1,0:T(8,128)(2,1)}, bf16[1024,2048]{1,0:T(8,128)(2,1)S(1)}, u32[]{:S(2)}) %copy-start) | copy-done | bytes 4194328
  32.5 8.6 %all-to-all-start = ((bf16[32,2,16,2048]{3,2,1,0:T(8,128)(2,1)}), bf16[32,2,16,2048]{3,2,1,0:T(8,128)(2,1)}, u32[]{:S(2)}, u32[]{:S(2)}) async-start(bf16[32,2,16,2048]{3,2,1,0:T(8,128)(2,1)} %bitcast.2), calls=%async_computation | async-start | bytes 8388608 | tf_op jit(solution)/shard_map/all_to_all | solution.py:158
  41.1 0.0 copy-done.5
  41.1 0.1 dynamic_slice.3.weight_ref
  41.2 52.1 %all-to-all-done.half_ref = bf16[32,2,16,2048]{3,2,1,0:T(8,128)(2,1)} async-done(((bf16[32,2,16,2048]{3,2,1,0:T(8,128)(2,1)}), bf16[32,2,16,2048]{3,2,1,0:T(8,128)(2,1)}, u32[]{:S(2)}, u32[]{:S(2)}) %all-to-all-start) | async-done | bytes 4194336 | tf_op jit(solution)/shard_map/all_to_all | solution.py:158
  93.3 0.0 copy-start.1
  93.3 3.4 %copy-done.1 = bf16[2048,2048]{1,0:T(8,128)(2,1)S(1)} copy-done((bf16[2048,2048]{1,0:T(8,128)(2,1)S(1)}, bf16[2048,2048]{1,0:T(8,128)(2,1)}, u32[]{:S(2)}) %copy-start.1) | copy-done | bytes 8388632
  96.7 17.0 %response.1 = bf16[512,512]{1,0:T(8,128)(2,1)S(1)} custom-call(f32[2]{0:T(128)S(1)} %dynamic_slice.3.weight_ref, bf16[32,2,16,2048]{3,2,1,0:T(8,128)(2,1)} %all-to-all-done.half_ref, bf16[2048,2048]{1,0:T(8,128)(2,1)S(1)} %copy-done.1), custom_call_target="tpu_custom_call" | custom-call | tf_op jit(solution)/shard_map/response/pallas_call | solution.py:131
  113.7 18.5 %all_to_all.10 = bf16[32,16,512]{2,1,0:T(8,128)(2,1)S(1)} all-to-all(bf16[32,16,512]{2,1,0:T(8,128)(2,1)S(1)} %bitcast.3), channel_id=1, replica_groups=mesh['rep'=4,'ten'=32] {'ten'}, dimensions={0} | all-to-all | bytes 1048576 | tf_op jit(solution)/shard_map/all_to_all | solution.py:161
  132.2 0.1 convert_reduce_fusion
  132.3 15.2 %psum.7 = f32[16,512]{1,0:T(8,128)} all-reduce(f32[16,512]{1,0:T(8,128)S(1)} %convert_reduce_fusion), channel_id=1, replica_groups=mesh['rep'=4,'ten'=32] {'rep'}, use_global_device_ids=true, to_apply=%region_1.0 | all-reduce | flops 8192 | bytes 65536 | tf_op jit(solution)/shard_map/psum | solution.py:163
Async XLA Ops:
  1.4 3.4 %copy-start.2 = (bf16[64,16,4096]{2,1,0:T(8,128)(2,1)S(1)}, bf16[64,16,4096]{2,1,0:T(8,128)(2,1)}, u32[]{:S(2)}) copy-start(bf16[64,16,4096]{2,1,0:T(8,128)(2,1)} %blocks_ref.1) | copy-start | bytes 25165828
  4.8 0.7 copy-start.3
  5.4 0.7 copy-start.4
  6.1 35.0 %copy-start.5 = (f32[64]{0:T(128)S(1)}, f32[64]{0:T(128)}, u32[]{:S(2)}) copy-start(f32[64]{0:T(128)} %param.10) | copy-start | bytes 772
  30.5 2.0 %copy-start = (bf16[1024,2048]{1,0:T(8,128)(2,1)}, bf16[1024,2048]{1,0:T(8,128)(2,1)S(1)}, u32[]{:S(2)}) copy-start(bf16[1024,2048]{1,0:T(8,128)(2,1)S(1)} %half_transform.1) | copy-start | bytes 12582916
  32.5 60.9 %all-to-all-start = ((bf16[32,2,16,2048]{3,2,1,0:T(8,128)(2,1)}), bf16[32,2,16,2048]{3,2,1,0:T(8,128)(2,1)}, u32[]{:S(2)}, u32[]{:S(2)}) async-start(bf16[32,2,16,2048]{3,2,1,0:T(8,128)(2,1)} %bitcast.2), calls=%async_computation | async-start | bytes 8388608 | tf_op jit(solution)/shard_map/all_to_all | solution.py:158
  93.3 3.4 %copy-start.1 = (bf16[2048,2048]{1,0:T(8,128)(2,1)S(1)}, bf16[2048,2048]{1,0:T(8,128)(2,1)}, u32[]{:S(2)}) copy-start(bf16[2048,2048]{1,0:T(8,128)(2,1)} %green_ref.1) | copy-start | bytes 25165828
where the time goes:
time: 150 us; the launch traced here: 148 us
  waiting for transfers between devices  52.1 us (35%)
  Pallas kernels  41.4 us (28%)
  blocking collectives  33.7 us (22%)
  local copies, waits for them, and re-layouts  11.5 us (8%)
  starting transfers between devices  8.65 us (6%)
    all_to_all x1, waiting for transfers between devices, per_device(): got = lax.all_to_all(half, 'ten', split_axis=0, concat_axis=0, tiled=True)  52.1 us
    pallas_call x1, Pallas kernels, half_transform(): pl.pallas_call(half_kernel, out_shape=jax.ShapeDtypeStruct((occ_count * a...  24.4 us
    all_to_all x1, blocking collectives, per_device(): lax.all_to_all(terms, 'ten', split_axis=0, concat_axis=0, tiled=True)  18.5 us
    pallas_call x1, Pallas kernels, response(): pl.pallas_call(response_kernel, grid=(basis_count // tile,), out_shape=ja...  17 us
    psum x1, blocking collectives, per_device(): return lax.psum(share, 'rep')  15.2 us
    unnamed x12, local copies, waits for them, and re-layouts  10 us
    all_to_all x1, starting transfers between devices, per_device(): got = lax.all_to_all(half, 'ten', split_axis=0, concat_axis=0, tiled=True)  8.65 us
  transfers between devices with their start and end apart: 1, of which 1 were waited for; matrix products, arithmetic and copies ran while one was open for 0% of the time, Pallas kernels for 0%

commit v1 on v0

v1 whole, which is shorter than its diff:
```python
import functools

import jax
import jax.numpy as jnp
from jax import lax
from jax.experimental import pallas as pl
from jax.experimental.pallas import tpu as pltpu
from jax.sharding import PartitionSpec as P

BS = 64
MOST = 4
LANES = 128
MIB = 1024 * 1024
BUFFERS = 3
CHUNKS = (6, 10)


def half_kernel(
    first_pair, pairs, counts_ref, sizes_ref, occ_ref, blocks_ref, out_ref, held, slots, turned, starts, sems
):
    block_count = counts_ref.shape[0]
    pair_count, aux_rows, _ = blocks_ref.shape
    occ_count = BS
    half_x = BS // 2
    pitch = half_x + 1
    turned_pitch = aux_rows + 1
    window = 2 * MOST

    def count_up(b, total):
        starts[b] = total
        return total + counts_ref[b]

    lax.fori_loop(0, 2 * (first_pair + pairs), count_up, jnp.int32(0))

    def base_of(m):
        return jnp.minimum(starts[2 * (first_pair + m)], pair_count - window)

    def fetch(m):
        slot = lax.rem(m, BUFFERS)
        return pltpu.make_async_copy(blocks_ref.at[pl.ds(base_of(m), window)], held.at[slot], sems.at[slot])

    for m in range(min(BUFFERS - 1, pairs)):
        fetch(jnp.int32(m)).start()
    slots[...] = jnp.zeros_like(slots)

    x_of = 2 * lax.broadcasted_iota(jnp.int32, (half_x, LANES), 0) + (
        lax.broadcasted_iota(jnp.int32, (half_x, LANES), 1) // BS
    )
    lane = lax.broadcasted_iota(jnp.int32, (BS, LANES), 1)
    low = lane < BS

    def column_pair(m, carry):
        @pl.when(m + BUFFERS - 1 < pairs)
        def _():
            fetch(m + BUFFERS - 1).start()

        fetch(m).wait()
        slot = lax.rem(m, BUFFERS)
        base = base_of(m)
        weights = []
        for side in range(2):
            b = 2 * (first_pair + m) + side
            first, count = starts[b] - base, counts_ref[b]
            rows = []
            for j in range(MOST):
                offset = (j + 1) // 2 if j % 2 == 1 else -(j // 2)
                row = lax.rem(b + offset + block_count, block_count)
                size = jnp.where(j < count, sizes_ref[row], 0)
                coeff = occ_ref[pl.ds(row * half_x, half_x), :]
                rows.append(jnp.where(x_of < size, coeff, 0.0))

                @pl.when(j < count)
                def _(side=side, j=j, first=first):
                    for t in range(half_x):
                        piece = held[slot, first + j, :, t * LANES : (t + 1) * LANES]
                        slots[side, j, pl.ds(t, aux_rows, stride=pitch), :] = piece.astype(jnp.float32)

            weights.append(jnp.transpose(jnp.concatenate(rows, axis=0)).astype(jnp.bfloat16))
        b = 2 * (first_pair + m)
        keep = lane < jnp.where(low, sizes_ref[b], sizes_ref[b + 1] + BS)
        for pp in range(aux_rows // 2):
            sums = []
            for side in range(2):
                cols = [
                    jnp.concatenate(
                        [slots[side, j, p * pitch : p * pitch + half_x, :] for j in range(MOST)], axis=0
                    ).astype(jnp.bfloat16)
                    for p in (2 * pp, 2 * pp + 1)
                ]
                sums.append(
                    jnp.dot(weights[side], jnp.concatenate(cols, axis=1), preferred_element_type=jnp.float32)
                )
            for q in range(2):
                even0 = sums[0][:BS, q * LANES : (q + 1) * LANES]
                odd0 = sums[0][BS:, q * LANES : (q + 1) * LANES]
                even1 = sums[1][:BS, q * LANES : (q + 1) * LANES]
                odd1 = sums[1][BS:, q * LANES : (q + 1) * LANES]
                total = jnp.where(low, even0, odd1) + pltpu.roll(jnp.where(low, even1, odd0), BS, 1)
                turned[pl.ds(2 * pp + q, occ_count, stride=turned_pitch), :] = jnp.where(keep, total, 0.0)
        for i in range(occ_count):
            out_ref[i * aux_rows : (i + 1) * aux_rows, pl.ds(pl.multiple_of(m * LANES, LANES), LANES)] = turned[
                i * turned_pitch : i * turned_pitch + aux_rows, :
            ].astype(jnp.bfloat16)
        return carry

    lax.fori_loop(0, pairs, column_pair, 0)


def half_transform(blocks, col_counts, block_sizes, occ, first_pair, pairs):
    pair_count, aux_rows, flat = blocks.shape
    block_count = col_counts.shape[0]
    occ_count = occ.shape[1] // 2
    smem = pl.BlockSpec(memory_space=pltpu.SMEM)
    vmem = pl.BlockSpec(memory_space=pltpu.VMEM)
    return pl.pallas_call(
        functools.partial(half_kernel, first_pair, pairs),
        out_shape=jax.ShapeDtypeStruct((occ_count * aux_rows, pairs * LANES), jnp.bfloat16),
        in_specs=[smem, smem, vmem, pl.BlockSpec(memory_space=pltpu.HBM)],
        out_specs=vmem,
        scratch_shapes=[
            pltpu.VMEM((BUFFERS, 2 * MOST, aux_rows, flat), jnp.bfloat16),
            pltpu.VMEM((2, MOST, aux_rows * (BS // 2 + 1), LANES), jnp.float32),
            pltpu.VMEM((occ_count * (aux_rows + 1), LANES), jnp.float32),
            pltpu.SMEM((block_count,), jnp.int32),
            pltpu.SemaphoreType.DMA((BUFFERS,)),
        ],
        compiler_params=pltpu.CompilerParams(vmem_limit_bytes=60 * MIB),
        cost_estimate=pl.CostEstimate(flops=pairs * 10**9, bytes_accessed=pairs * MIB, transcendentals=0),
        name="half_transform",
    )(col_counts, block_sizes, occ, blocks)


def dress_kernel(half_ref, green_ref, out_ref):
    sources, own, aux_rows, depth = half_ref.shape
    rows = sources * aux_rows
    for ii in range(own):
        out_ref[ii] = jnp.dot(
            half_ref[:, ii].reshape(rows, depth), green_ref[...], preferred_element_type=jnp.float32
        )


def dress(half, virt_green, first, tile=256):
    sources, own, aux_rows, depth = half.shape
    rows = sources * aux_rows
    basis_count = virt_green.shape[1]
    return pl.pallas_call(
        dress_kernel,
        grid=(basis_count // tile,),
        out_shape=jax.ShapeDtypeStruct((own, rows, basis_count), jnp.float32),
        in_specs=[
            pl.BlockSpec((sources, own, aux_rows, depth), lambda n: (0, 0, 0, 0)),
            pl.BlockSpec((pl.Element(depth), pl.Element(tile)), lambda n: (first, n * tile)),
        ],
        out_specs=pl.BlockSpec((own, rows, tile), lambda n: (0, 0, n)),
        compiler_params=pltpu.CompilerParams(vmem_limit_bytes=60 * MIB),
        cost_estimate=pl.CostEstimate(
            flops=2 * own * rows * depth * basis_count,
            bytes_accessed=2 * own * rows * depth + 2 * depth * basis_count + 4 * own * rows * basis_count,
            transcendentals=0,
        ),
        name="dress",
    )(half, virt_green)


def response_kernel(split, weight_ref, half0_ref, half1_ref, green_ref, part_ref, chi_ref, total):
    step = pl.program_id(0)
    sources, own, aux_rows, depth = half1_ref.shape
    rows = sources * aux_rows
    tile = green_ref.shape[1]

    @pl.when(step == 0)
    def _():
        total[...] = jnp.zeros_like(total)

    def add(half_ref, columns):
        for ii in range(own):
            dressed = part_ref[ii] + jnp.dot(
                half1_ref[:, ii].reshape(rows, depth), green_ref[...], preferred_element_type=jnp.float32
            )
            dressed = (dressed * weight_ref[ii]).astype(jnp.bfloat16)
            left = half_ref[:, ii, :, columns].reshape(rows, tile)
            total[...] += lax.dot_general(
                left, dressed, (((1,), (1,)), ((), ())), preferred_element_type=jnp.float32
            )

    @pl.when(step < split)
    def _():
        add(half0_ref, pl.ds(pl.multiple_of(step * tile, tile), tile))

    @pl.when(step >= split)
    def _():
        add(half1_ref, pl.ds(pl.multiple_of((step - split) * tile, tile), tile))

    @pl.when(step == pl.num_programs(0) - 1)
    def _():
        chi_ref[...] = total[...].astype(chi_ref.dtype)


def response(half0, half1, weight, part, virt_green, tile=256):
    sources, own, aux_rows, depth0 = half0.shape
    depth1 = half1.shape[3]
    rows = sources * aux_rows
    basis_count = virt_green.shape[1]
    whole = lambda n: (0, 0, 0, 0)
    return pl.pallas_call(
        functools.partial(response_kernel, depth0 // tile),
        grid=(basis_count // tile,),
        out_shape=jax.ShapeDtypeStruct((rows, rows), jnp.bfloat16),
        in_specs=[
            pl.BlockSpec(memory_space=pltpu.SMEM),
            pl.BlockSpec((sources, own, aux_rows, depth0), whole),
            pl.BlockSpec((sources, own, aux_rows, depth1), whole),
            pl.BlockSpec((pl.Element(depth1), pl.Element(tile)), lambda n: (depth0, n * tile)),
            pl.BlockSpec((own, rows, tile), lambda n: (0, 0, n)),
        ],
        out_specs=pl.BlockSpec((rows, rows), lambda n: (0, 0)),
        scratch_shapes=[pltpu.VMEM((rows, rows), jnp.float32)],
        compiler_params=pltpu.CompilerParams(vmem_limit_bytes=60 * MIB),
        name="response",
    )(weight, half0, half1, virt_green, part)


def per_device(blocks, col_counts, block_sizes, occ_coeff, occ_weight, virt_green):
    devices = lax.axis_size("ten")
    aux_rows = blocks.shape[1]
    occ_count = occ_coeff.shape[1]
    own = occ_count // devices
    occ = occ_coeff.astype(jnp.float32).reshape(devices * BS // 2, 2 * occ_count)
    got, first = [], 0
    for pairs in CHUNKS:
        half = half_transform(blocks, col_counts, block_sizes, occ, first, pairs)
        half = half.reshape(devices, own, aux_rows, pairs * LANES)
        got.append(lax.all_to_all(half, "ten", split_axis=0, concat_axis=0, tiled=True))
        first += pairs
    weight = lax.dynamic_slice(occ_weight, (lax.axis_index("ten") * own,), (own,))
    part = dress(got[0], virt_green, 0)
    terms = response(got[0], got[1], weight, part, virt_green).reshape(devices, aux_rows, devices * aux_rows)
    terms = lax.all_to_all(terms, "ten", split_axis=0, concat_axis=0, tiled=True)
    share = jnp.sum(terms.astype(jnp.float32), axis=0)
    groups = lax.axis_size("rep")
    one, two, three = (
        lax.ppermute(share, "rep", [(z, (z + step) % groups) for z in range(groups)]) for step in (1, 2, 3)
    )
    return (share + two) + (one + three)


def solution(mesh):
    return jax.shard_map(
        per_device,
        mesh=mesh,
        in_specs=(P(None, "ten", None), P(), P(), P(None, "rep"), P("rep"), P()),
        out_specs=P("ten", None),
        check_vma=False,
    )
```

time: 150 us -> 122 us (0.81); the launches traced: 148 us -> 121 us
  blocking collectives: 33.7 us -> 16.3 us
  waiting for transfers between devices: 52.1 us -> 37.9 us
  starting transfers between devices: 8.65 us -> 18.8 us
  local copies, waits for them, and re-layouts: 11.5 us -> 3.9 us
  Pallas kernels: 41.4 us -> 43.5 us
    all_to_all x1 -> x2, waiting for transfers between devices: 52.1 us -> 34.9 us  [per_device(): lax.all_to_all(half, 'ten', split_axis=0, concat_axis=0, tiled=True)]
    psum x1 -> x0, blocking collectives: 15.2 us -> none  [per_device(): return lax.psum(share, 'rep')]
    unnamed x12 -> x4, local copies, waits for them, and re-layouts: 10 us -> 1.15 us
    ppermute x0 -> x3, starting transfers between devices: none -> 5.14 us  [per_device(): lax.ppermute(share, 'rep', [(z, (z + step) % groups) for z in range(group...]
    all_to_all x1 -> x2, starting transfers between devices: 8.65 us -> 13.7 us  [per_device(): lax.all_to_all(half, 'ten', split_axis=0, concat_axis=0, tiled=True)]
    ppermute x0 -> x3, waiting for transfers between devices: none -> 3.04 us  [per_device(): lax.ppermute(share, 'rep', [(z, (z + step) % groups) for z in range(group...]
    all_to_all x1, blocking collectives: 18.5 us -> 16.3 us  [per_device(): lax.all_to_all(terms, 'ten', split_axis=0, concat_axis=0, tiled=True)]
    pallas_call x2 -> x4, Pallas kernels: 41.4 us -> 43.5 us  [the longest x2 19.5 us: half_transform(): pl.pallas_call(functools.partial(half_kernel, first_pair, pairs), out_sha...]
  transfers between devices with their start and end apart: 1 -> 5, of which waited for: 1 -> 4; matrix products, arithmetic and copies ran while one was open for 0% -> 0% of each run, Pallas kernels for 0% -> 18%
where the time goes in v1:
time: 122 us; the launch traced here: 121 us
  Pallas kernels  43.5 us (36%)
  waiting for transfers between devices  37.9 us (31%)
  starting transfers between devices  18.8 us (15%)
  blocking collectives  16.3 us (13%)
  local copies, waits for them, and re-layouts  3.9 us (3%)
    all_to_all x2, waiting for transfers between devices, per_device(): lax.all_to_all(half, 'ten', split_axis=0, concat_axis=0, tiled=True)  34.9 us
    pallas_call x2, Pallas kernels, half_transform(): pl.pallas_call(functools.partial(half_kernel, first_pair, pairs), out_sha...  19.5 us
    all_to_all x1, blocking collectives, per_device(): lax.all_to_all(terms, 'ten', split_axis=0, concat_axis=0, tiled=True)  16.3 us
    pallas_call x1, Pallas kernels, response(): pl.pallas_call(functools.partial(response_kernel, depth0 // tile), grid=(...  14.3 us
    all_to_all x2, starting transfers between devices, per_device(): lax.all_to_all(half, 'ten', split_axis=0, concat_axis=0, tiled=True)  13.7 us
    pallas_call x1, Pallas kernels, dress(): pl.pallas_call(dress_kernel, grid=(basis_count // tile,), out_shape=jax.S...  9.74 us
    ppermute x3, starting transfers between devices, per_device(): lax.ppermute(share, 'rep', [(z, (z + step) % groups) for z in range(group...  5.14 us
    ppermute x3, waiting for transfers between devices, per_device(): lax.ppermute(share, 'rep', [(z, (z + step) % groups) for z in range(group...  3.04 us
  transfers between devices with their start and end apart: 5, of which 4 were waited for; matrix products, arithmetic and copies ran while one was open for 0% of the time, Pallas kernels for 18%

profile of v1, /device:TPU:1, one launch (start us, length us, event | category | flops | bytes accessed | tf_op | source)
XLA Modules:
  0.0 121.2 jit_solution(13608297412538906283)
XLA Ops:
  0.0 1.2 copy.8
  1.2 1.0 reshape.20.occ_ref
  2.2 8.0 %half_transform.2 = bf16[1024,768]{1,0:T(8,128)(2,1)} custom-call(s32[32]{0:T(128)} %counts_ref.3, s32[32]{0:T(128)} %sizes_ref.3, f32[1024,128]{1,0:T(8,128)} %reshape.20.occ_ref, bf16[64,16,4096]{2,1,0:T(8,128)(2,1)} %blocks_ref.3), custom_call_target="tpu_custom_call" | custom-call | flops 6000000000 | bytes 6291456 | tf_op jit(solution)/shard_map/half_transform/pallas_call | solution.py:115
  10.2 8.6 %all-to-all-start = ((bf16[32,2,16,768]{3,2,1,0:T(8,128)(2,1)}), bf16[32,2,16,768]{3,2,1,0:T(8,128)(2,1)S(1)}, u32[]{:S(2)}, u32[]{:S(2)}) async-start(bf16[32,2,16,768]{3,2,1,0:T(8,128)(2,1)} %bitcast.5), calls=%async_computation | async-start | bytes 3145728 | tf_op jit(solution)/shard_map/all_to_all | solution.py:233
  18.8 11.5 %half_transform.3 = bf16[1024,1280]{1,0:T(8,128)(2,1)} custom-call(s32[32]{0:T(128)} %counts_ref.3, s32[32]{0:T(128)} %sizes_ref.3, f32[1024,128]{1,0:T(8,128)} %reshape.20.occ_ref, bf16[64,16,4096]{2,1,0:T(8,128)(2,1)} %blocks_ref.3), custom_call_target="tpu_custom_call" | custom-call | flops 10000000000 | bytes 10485760 | tf_op jit(solution)/shard_map/half_transform/pallas_call | solution.py:115
  30.3 11.2 %all-to-all-done.half_ref.half0_ref = bf16[32,2,16,768]{3,2,1,0:T(8,128)(2,1)S(1)} async-done(((bf16[32,2,16,768]{3,2,1,0:T(8,128)(2,1)}), bf16[32,2,16,768]{3,2,1,0:T(8,128)(2,1)S(1)}, u32[]{:S(2)}, u32[]{:S(2)}) %all-to-all-start) | async-done | bytes 1572896 | tf_op jit(solution)/shard_map/all_to_all | solution.py:233
  41.5 0.0 copy-start
  41.5 0.0 copy-start.1
  41.5 1.1 copy-done
  42.6 5.1 %all-to-all-start.1 = ((bf16[32,2,16,1280]{3,2,1,0:T(8,128)(2,1)}), bf16[32,2,16,1280]{3,2,1,0:T(8,128)(2,1)}, u32[]{:S(2)}, u32[]{:S(2)}) async-start(bf16[32,2,16,1280]{3,2,1,0:T(8,128)(2,1)} %bitcast.3), calls=%async_computation.1 | async-start | bytes 5242880 | tf_op jit(solution)/shard_map/all_to_all | solution.py:233
  47.7 0.0 copy-done.1
  47.7 0.6 dynamic_slice.3.weight_ref
  48.3 9.7 %dress.1.part_ref = f32[2,512,2048]{2,1,0:T(8,128)} custom-call(bf16[32,2,16,768]{3,2,1,0:T(8,128)(2,1)} %copy-done, bf16[2048,2048]{1,0:T(8,128)(2,1)} %green_ref.3), custom_call_target="tpu_custom_call" | custom-call | flops 3221225472 | bytes 13107200 | tf_op jit(solution)/shard_map/dress/pallas_call | solution.py:146
  58.1 23.7 %all-to-all-done.1.half1_ref = bf16[32,2,16,1280]{3,2,1,0:T(8,128)(2,1)} async-done(((bf16[32,2,16,1280]{3,2,1,0:T(8,128)(2,1)}), bf16[32,2,16,1280]{3,2,1,0:T(8,128)(2,1)}, u32[]{:S(2)}, u32[]{:S(2)}) %all-to-all-start.1) | async-done | bytes 2621472 | tf_op jit(solution)/shard_map/all_to_all | solution.py:233
  81.8 14.3 %response.1 = bf16[512,512]{1,0:T(8,128)(2,1)} custom-call(f32[2]{0:T(128)} %dynamic_slice.3.weight_ref, bf16[32,2,16,768]{3,2,1,0:T(8,128)(2,1)} %copy-done, bf16[32,2,16,1280]{3,2,1,0:T(8,128)(2,1)} %all-to-all-done.1.half1_ref, bf16[2048,2048]{1,0:T(8,128)(2,1)} %green_ref.3, f32[2,512,2048]{2,1,0:T(8,128)} %dress.1.part_ref), custom_call_target="tpu_custom_call" | custom-call | tf_op jit(solution)/shard_map/response/pallas_call | solution.py:205
  96.1 16.3 %all_to_all.15 = bf16[32,16,512]{2,1,0:T(8,128)(2,1)S(1)} all-to-all(bf16[32,16,512]{2,1,0:T(8,128)(2,1)} %bitcast.4), channel_id=1, replica_groups=mesh['rep'=4,'ten'=32] {'ten'}, dimensions={0} | all-to-all | bytes 1048576 | tf_op jit(solution)/shard_map/all_to_all | solution.py:238
  112.3 0.1 convert_reduce_fusion
  112.4 3.8 %collective-permute-start.2 = (f32[16,512]{1,0:T(8,128)S(1)}, f32[16,512]{1,0:T(8,128)S(1)}, u32[]{:S(2)}, u32[]{:S(2)}) collective-permute-start(f32[16,512]{1,0:T(8,128)S(1)} %convert_reduce_fusion), channel_id=1, source_target_pairs={{0,96},{32,0},{64,32},{96,64},{1,97},{33,1},{65,33},{97,65},{2,98}... | collective-permute-start | bytes 98312 | tf_op jit(solution)/shard_map/ppermute | solution.py:242
  116.2 0.0 collective-permute-start.1
  116.3 1.3 %collective-permute-start = (f32[16,512]{1,0:T(8,128)S(1)}, f32[16,512]{1,0:T(8,128)S(1)}, u32[]{:S(2)}, u32[]{:S(2)}) collective-permute-start(f32[16,512]{1,0:T(8,128)S(1)} %convert_reduce_fusion), channel_id=1, source_target_pairs={{0,64},{32,96},{64,0},{96,32},{1,65},{33,97},{65,1},{97,33},{2,66}... | collective-permute-start | bytes 98312 | tf_op jit(solution)/shard_map/ppermute | solution.py:242
  117.6 0.0 collective-permute-done.2
  117.6 2.7 %collective-permute-done.1 = f32[16,512]{1,0:T(8,128)S(1)} collective-permute-done((f32[16,512]{1,0:T(8,128)S(1)}, f32[16,512]{1,0:T(8,128)S(1)}, u32[]{:S(2)}, u32[]{:S(2)}) %collective-permute-start.1) | collective-permute-done | bytes 32800 | tf_op jit(solution)/shard_map/ppermute | solution.py:242
  120.2 0.4 collective-permute-done
  120.6 0.6 add_add_fusion
Async XLA Ops:
  10.2 31.3 %all-to-all-start = ((bf16[32,2,16,768]{3,2,1,0:T(8,128)(2,1)}), bf16[32,2,16,768]{3,2,1,0:T(8,128)(2,1)S(1)}, u32[]{:S(2)}, u32[]{:S(2)}) async-start(bf16[32,2,16,768]{3,2,1,0:T(8,128)(2,1)} %bitcast.5), calls=%async_computation | async-start | bytes 3145728 | tf_op jit(solution)/shard_map/all_to_all | solution.py:233
  41.5 1.2 copy-start
  41.5 6.3 %copy-start.1 = (f32[64]{0:T(128)S(1)}, f32[64]{0:T(128)}, u32[]{:S(2)}) copy-start(f32[64]{0:T(128)} %param.10) | copy-start | bytes 772
  42.6 39.1 %all-to-all-start.1 = ((bf16[32,2,16,1280]{3,2,1,0:T(8,128)(2,1)}), bf16[32,2,16,1280]{3,2,1,0:T(8,128)(2,1)}, u32[]{:S(2)}, u32[]{:S(2)}) async-start(bf16[32,2,16,1280]{3,2,1,0:T(8,128)(2,1)} %bitcast.3), calls=%async_computation.1 | async-start | bytes 5242880 | tf_op jit(solution)/shard_map/all_to_all | solution.py:233
  112.4 5.1 %collective-permute-start.2 = (f32[16,512]{1,0:T(8,128)S(1)}, f32[16,512]{1,0:T(8,128)S(1)}, u32[]{:S(2)}, u32[]{:S(2)}) collective-permute-start(f32[16,512]{1,0:T(8,128)S(1)} %convert_reduce_fusion), channel_id=1, source_target_pairs={{0,96},{32,0},{64,32},{96,64},{1,97},{33,1},{65,33},{97,65},{2,98}... | collective-permute-start | bytes 98312 | tf_op jit(solution)/shard_map/ppermute | solution.py:242
  116.2 4.0 %collective-permute-start.1 = (f32[16,512]{1,0:T(8,128)S(1)}, f32[16,512]{1,0:T(8,128)S(1)}, u32[]{:S(2)}, u32[]{:S(2)}) collective-permute-start(f32[16,512]{1,0:T(8,128)S(1)} %convert_reduce_fusion), channel_id=1, source_target_pairs={{0,32},{32,64},{64,96},{96,0},{1,33},{33,65},{65,97},{97,1},{2,34}... | collective-permute-start | bytes 98312 | tf_op jit(solution)/shard_map/ppermute | solution.py:242
  116.3 4.4 %collective-permute-start = (f32[16,512]{1,0:T(8,128)S(1)}, f32[16,512]{1,0:T(8,128)S(1)}, u32[]{:S(2)}, u32[]{:S(2)}) collective-permute-start(f32[16,512]{1,0:T(8,128)S(1)} %convert_reduce_fusion), channel_id=1, source_target_pairs={{0,64},{32,96},{64,0},{96,32},{1,65},{33,97},{65,1},{97,33},{2,66}... | collective-permute-start | bytes 98312 | tf_op jit(solution)/shard_map/ppermute | solution.py:242

commit v2 on v1

v2 whole, which is shorter than its diff:
```python
import functools

import jax
import jax.numpy as jnp
from jax import lax
from jax.experimental import pallas as pl
from jax.experimental.pallas import tpu as pltpu
from jax.sharding import PartitionSpec as P

BS = 64
MOST = 4
LANES = 128
MIB = 1024 * 1024
BUFFERS = 3
WIDTHS = (12, 13, 14, 16)
FIRST = 4


def prefix_sums(counts_ref, into):
    def count_up(b, total):
        into[b] = total
        return total + counts_ref[b]

    return lax.fori_loop(0, counts_ref.shape[0], count_up, jnp.int32(0))


def targets(position, sizes_ref, offsets, m):
    size0, size1 = sizes_ref[2 * m], sizes_ref[2 * m + 1]
    start = offsets[2 * m]
    second = position >= BS
    local = jnp.where(second, position - BS, position)
    place = (local + jnp.where(second, start + size0, start)) & (LANES - 1)
    return jnp.where(local < jnp.where(second, size1, size0), place, -1)


def half_kernel(
    lo, hi, counts_ref, sizes_ref, occ_ref, blocks_ref, out_ref,
    held, slots, turned, carry, starts, offsets, sems,
):
    block_count = counts_ref.shape[0]
    pair_count, aux_rows, _ = blocks_ref.shape
    occ_count = occ_ref.shape[1]
    half_x = BS // 2
    pitch = half_x + 1
    turned_pitch = aux_rows + 1
    window = 2 * MOST
    last_pair = block_count // 2

    prefix_sums(counts_ref, starts)
    used = prefix_sums(sizes_ref, offsets)

    def count_before(limit):
        return lax.fori_loop(
            0, last_pair, lambda m, n: n + (offsets[2 * m] < limit).astype(jnp.int32), jnp.int32(0)
        )

    m_lo = jnp.int32(0) if lo == 0 else count_before(lo * LANES + 1) - 1
    m_hi = count_before(hi * LANES)

    def base_of(m):
        return jnp.minimum(starts[2 * m], pair_count - window)

    def fetch(m):
        slot = lax.rem(m, BUFFERS)
        return pltpu.make_async_copy(blocks_ref.at[pl.ds(base_of(m), window)], held.at[slot], sems.at[slot])

    for ahead in range(BUFFERS - 1):

        @pl.when(m_lo + ahead < m_hi)
        def _(ahead=ahead):
            fetch(m_lo + ahead).start()

    slots[...] = jnp.zeros_like(slots)
    carry[...] = jnp.zeros_like(carry)

    twice = 2 * lax.broadcasted_iota(jnp.int32, (half_x, occ_count), 0)
    low = lax.broadcasted_iota(jnp.int32, (BS, LANES), 1) < BS
    square_row = lax.broadcasted_iota(jnp.int32, (LANES, LANES), 0)
    square_lane = lax.broadcasted_iota(jnp.int32, (LANES, LANES), 1)

    def column_pair(m, state):
        @pl.when(m + BUFFERS - 1 < m_hi)
        def _():
            fetch(m + BUFFERS - 1).start()

        fetch(m).wait()
        slot = lax.rem(m, BUFFERS)
        base = base_of(m)
        weights = []
        for side in range(2):
            b = 2 * m + side
            first, count = starts[b] - base, counts_ref[b]
            rows = [[], []]
            for j in range(MOST):
                offset = (j + 1) // 2 if j % 2 == 1 else -(j // 2)
                row = lax.rem(b + offset + block_count, block_count)
                size = jnp.where(j < count, sizes_ref[row], 0)
                for parity in range(2):
                    coeff = occ_ref[pl.ds(row * BS + parity, half_x, stride=2), :]
                    rows[parity].append(jnp.where(twice + parity < size, coeff, 0.0))

                @pl.when(j < count)
                def _(side=side, j=j, first=first):
                    for t in range(half_x):
                        piece = held[slot, first + j, :, t * LANES : (t + 1) * LANES]
                        slots[side, j, pl.ds(t, aux_rows, stride=pitch), :] = piece.astype(jnp.float32)

            weights.append(
                jnp.concatenate(
                    [jnp.transpose(jnp.concatenate(part, axis=0)) for part in rows], axis=0
                ).astype(jnp.bfloat16)
            )
        for pp in range(aux_rows // 2):
            sums = []
            for side in range(2):
                cols = [
                    jnp.concatenate(
                        [slots[side, j, p * pitch : p * pitch + half_x, :] for j in range(MOST)], axis=0
                    ).astype(jnp.bfloat16)
                    for p in (2 * pp, 2 * pp + 1)
                ]
                sums.append(
                    jnp.dot(weights[side], jnp.concatenate(cols, axis=1), preferred_element_type=jnp.float32)
                )
            for q in range(2):
                even0 = sums[0][:BS, q * LANES : (q + 1) * LANES]
                odd0 = sums[0][BS:, q * LANES : (q + 1) * LANES]
                even1 = sums[1][:BS, q * LANES : (q + 1) * LANES]
                odd1 = sums[1][BS:, q * LANES : (q + 1) * LANES]
                turned[pl.ds(2 * pp + q, occ_count, stride=turned_pitch), :] = jnp.where(
                    low, even0, odd1
                ) + pltpu.roll(jnp.where(low, even1, odd0), BS, 1)

        start = offsets[2 * m]
        tile, split = start // LANES, start % LANES
        filled = split + sizes_ref[2 * m] + sizes_ref[2 * m + 1]
        full = filled >= LANES
        select = (square_lane == targets(square_row, sizes_ref, offsets, m)).astype(jnp.bfloat16)
        here = square_lane >= split
        column = pl.ds(pl.multiple_of(jnp.maximum(tile - lo, 0) * LANES, LANES), LANES)
        group = LANES // aux_rows
        for g in range(occ_count // group):
            values = jnp.concatenate(
                [turned[i * turned_pitch : i * turned_pitch + aux_rows, :] for i in range(g * group, (g + 1) * group)],
                axis=0,
            ).astype(jnp.bfloat16)
            moved = jnp.dot(values, select, preferred_element_type=jnp.float32)
            rows = slice(g * LANES, (g + 1) * LANES)
            current = carry[rows, :] + jnp.where(here, moved, 0.0)
            out_ref[rows, column] = current.astype(jnp.bfloat16)
            carry[rows, :] = jnp.where(full, jnp.where(here, 0.0, moved), current)
        return jnp.where(filled > LANES, tile + 1, -1)

    spill = lax.fori_loop(m_lo, m_hi, column_pair, jnp.int32(-1))

    def zero(tile, state):
        out_ref[:, pl.ds(pl.multiple_of((tile - lo) * LANES, LANES), LANES)] = jnp.zeros(
            (out_ref.shape[0], LANES), jnp.bfloat16
        )
        return state

    lax.fori_loop(jnp.maximum((used + LANES - 1) // LANES, lo), hi, zero, 0)

    @pl.when((spill >= lo) & (spill < hi))
    def _():
        out_ref[:, pl.ds(pl.multiple_of((spill - lo) * LANES, LANES), LANES)] = carry[...].astype(jnp.bfloat16)


def half_transform(blocks, col_counts, block_sizes, occ, lo, hi):
    pair_count, aux_rows, flat = blocks.shape
    block_count = col_counts.shape[0]
    occ_count = occ.shape[1]
    smem = pl.BlockSpec(memory_space=pltpu.SMEM)
    vmem = pl.BlockSpec(memory_space=pltpu.VMEM)
    return pl.pallas_call(
        functools.partial(half_kernel, lo, hi),
        out_shape=jax.ShapeDtypeStruct((occ_count * aux_rows, (hi - lo) * LANES), jnp.bfloat16),
        in_specs=[smem, smem, vmem, pl.BlockSpec(memory_space=pltpu.HBM)],
        out_specs=vmem,
        scratch_shapes=[
            pltpu.VMEM((BUFFERS, 2 * MOST, aux_rows, flat), jnp.bfloat16),
            pltpu.VMEM((2, MOST, aux_rows * (BS // 2 + 1), LANES), jnp.float32),
            pltpu.VMEM((occ_count * (aux_rows + 1), LANES), jnp.float32),
            pltpu.VMEM((occ_count * aux_rows, LANES), jnp.float32),
            pltpu.SMEM((block_count,), jnp.int32),
            pltpu.SMEM((block_count,), jnp.int32),
            pltpu.SemaphoreType.DMA((BUFFERS,)),
        ],
        compiler_params=pltpu.CompilerParams(vmem_limit_bytes=60 * MIB),
        cost_estimate=pl.CostEstimate(flops=(hi - lo) * 10**9, bytes_accessed=(hi - lo) * MIB, transcendentals=0),
        name="half_transform",
    )(col_counts, block_sizes, occ, blocks)


def pack_kernel(sizes_ref, green_ref, out_ref, packed_rows, row_carry, lane_carry, offsets):
    basis_count = green_ref.shape[0]
    width = out_ref.shape[0]
    last_pair = sizes_ref.shape[0] // 2
    used = prefix_sums(sizes_ref, offsets)
    tiles = (used + LANES - 1) // LANES
    square_row = lax.broadcasted_iota(jnp.int32, (LANES, LANES), 0)
    square_lane = lax.broadcasted_iota(jnp.int32, (LANES, LANES), 1)
    strip = 4 * LANES
    row_carry[...] = jnp.zeros_like(row_carry)
    lane_carry[...] = jnp.zeros_like(lane_carry)

    def place(m):
        start = offsets[2 * m]
        split = start % LANES
        return start // LANES, split, split + sizes_ref[2 * m] + sizes_ref[2 * m + 1]

    def at(tile):
        return pl.ds(pl.multiple_of(tile * LANES, LANES), LANES)

    def pack_rows(m, state):
        tile, split, filled = place(m)
        select = (square_row == targets(square_lane, sizes_ref, offsets, m)).astype(jnp.bfloat16)
        here = lax.broadcasted_iota(jnp.int32, (LANES, strip), 0) >= split
        for s in range(basis_count // strip):
            lanes = slice(s * strip, (s + 1) * strip)
            moved = jnp.dot(select, green_ref[at(m), lanes], preferred_element_type=jnp.float32)
            current = row_carry[:, lanes] + jnp.where(here, moved, 0.0)
            packed_rows[at(tile), lanes] = current.astype(jnp.bfloat16)
            row_carry[:, lanes] = jnp.where(filled >= LANES, jnp.where(here, 0.0, moved), current)
        return jnp.where(filled > LANES, tile + 1, -1)

    spill = lax.fori_loop(0, last_pair, pack_rows, jnp.int32(-1))

    def zero_rows(tile, state):
        packed_rows[at(tile), :] = jnp.zeros((LANES, basis_count), jnp.bfloat16)
        return state

    lax.fori_loop(tiles, width // LANES, zero_rows, 0)

    @pl.when(spill >= 0)
    def _():
        packed_rows[at(spill), :] = row_carry[...].astype(jnp.bfloat16)

    def pack_lanes(m, state):
        tile, split, filled = place(m)
        select = (square_lane == targets(square_row, sizes_ref, offsets, m)).astype(jnp.bfloat16)
        here = square_lane >= split
        for r in range(width // LANES):
            rows = slice(r * LANES, (r + 1) * LANES)
            moved = jnp.dot(packed_rows[rows, at(m)], select, preferred_element_type=jnp.float32)
            current = lane_carry[rows, :] + jnp.where(here, moved, 0.0)
            out_ref[rows, at(tile)] = current.astype(jnp.bfloat16)
            lane_carry[rows, :] = jnp.where(filled >= LANES, jnp.where(here, 0.0, moved), current)
        return state

    lax.fori_loop(0, last_pair, pack_lanes, 0)

    def zero_lanes(tile, state):
        out_ref[:, at(tile)] = jnp.zeros((width, LANES), jnp.bfloat16)
        return state

    lax.fori_loop(tiles, width // LANES, zero_lanes, 0)

    @pl.when(spill >= 0)
    def _():
        out_ref[:, at(spill)] = lane_carry[...].astype(jnp.bfloat16)


def pack_green(block_sizes, virt_green, width):
    basis_count = virt_green.shape[0]
    vmem = pl.BlockSpec(memory_space=pltpu.VMEM)
    return pl.pallas_call(
        pack_kernel,
        out_shape=jax.ShapeDtypeStruct((width, width), jnp.bfloat16),
        in_specs=[pl.BlockSpec(memory_space=pltpu.SMEM), vmem],
        out_specs=vmem,
        scratch_shapes=[
            pltpu.VMEM((width, basis_count), jnp.bfloat16),
            pltpu.VMEM((LANES, basis_count), jnp.float32),
            pltpu.VMEM((width, LANES), jnp.float32),
            pltpu.SMEM((block_sizes.shape[0],), jnp.int32),
        ],
        compiler_params=pltpu.CompilerParams(vmem_limit_bytes=60 * MIB),
        cost_estimate=pl.CostEstimate(flops=10 * 10**9, bytes_accessed=14 * MIB, transcendentals=0),
        name="pack_green",
    )(block_sizes, virt_green)


def dress_kernel(half_ref, green_ref, out_ref):
    sources, own, aux_rows, depth = half_ref.shape
    rows = sources * aux_rows
    for ii in range(own):
        out_ref[ii] = jnp.dot(
            half_ref[:, ii].reshape(rows, depth), green_ref[...], preferred_element_type=jnp.float32
        )


def column_start(step, tile, width):
    return pl.multiple_of(jnp.minimum(step * tile, width - tile), LANES)


def dress(half, green, tile=256):
    sources, own, aux_rows, depth = half.shape
    rows = sources * aux_rows
    width = green.shape[1]
    steps = pl.cdiv(width, tile)
    return pl.pallas_call(
        dress_kernel,
        grid=(steps,),
        out_shape=jax.ShapeDtypeStruct((own, rows, steps * tile), jnp.float32),
        in_specs=[
            pl.BlockSpec((sources, own, aux_rows, depth), lambda n: (0, 0, 0, 0)),
            pl.BlockSpec((pl.Element(depth), pl.Element(tile)), lambda n: (0, column_start(n, tile, width))),
        ],
        out_specs=pl.BlockSpec((own, rows, tile), lambda n: (0, 0, n)),
        compiler_params=pltpu.CompilerParams(vmem_limit_bytes=60 * MIB),
        cost_estimate=pl.CostEstimate(
            flops=2 * own * rows * depth * width,
            bytes_accessed=2 * own * rows * depth + 2 * depth * width + 4 * own * rows * width,
            transcendentals=0,
        ),
        name="dress",
    )(half, green)


def response_kernel(split, width, weight_ref, half0_ref, half1_ref, green_ref, part_ref, chi_ref, total):
    step = pl.program_id(0)
    sources, own, aux_rows, depth = half1_ref.shape
    rows = sources * aux_rows
    tile = green_ref.shape[1]
    start = column_start(step, tile, width)
    fresh = lax.broadcasted_iota(jnp.int32, (rows, tile), 1) >= step * tile - start

    @pl.when(step == 0)
    def _():
        total[...] = jnp.zeros_like(total)

    def add(half_ref, first):
        columns = pl.ds(pl.multiple_of(start - first, LANES), tile)
        for ii in range(own):
            dressed = part_ref[ii] + jnp.dot(
                half1_ref[:, ii].reshape(rows, depth), green_ref[...], preferred_element_type=jnp.float32
            )
            dressed = jnp.where(fresh, dressed * weight_ref[ii], 0.0).astype(jnp.bfloat16)
            left = half_ref[:, ii, :, columns].reshape(rows, tile)
            total[...] += lax.dot_general(
                left, dressed, (((1,), (1,)), ((), ())), preferred_element_type=jnp.float32
            )

    @pl.when(step < split // tile)
    def _():
        add(half0_ref, 0)

    @pl.when(step >= split // tile)
    def _():
        add(half1_ref, split)

    @pl.when(step == pl.num_programs(0) - 1)
    def _():
        chi_ref[...] = total[...].astype(chi_ref.dtype)


def response(half0, half1, weight, part, green, tile=256):
    sources, own, aux_rows, depth0 = half0.shape
    depth1 = half1.shape[3]
    rows = sources * aux_rows
    width = depth0 + depth1
    whole = lambda n: (0, 0, 0, 0)
    return pl.pallas_call(
        functools.partial(response_kernel, depth0, width),
        grid=(pl.cdiv(width, tile),),
        out_shape=jax.ShapeDtypeStruct((rows, rows), jnp.bfloat16),
        in_specs=[
            pl.BlockSpec(memory_space=pltpu.SMEM),
            pl.BlockSpec((sources, own, aux_rows, depth0), whole),
            pl.BlockSpec((sources, own, aux_rows, depth1), whole),
            pl.BlockSpec((pl.Element(depth1), pl.Element(tile)), lambda n: (depth0, column_start(n, tile, width))),
            pl.BlockSpec((own, rows, tile), lambda n: (0, 0, n)),
        ],
        out_specs=pl.BlockSpec((rows, rows), lambda n: (0, 0)),
        scratch_shapes=[pltpu.VMEM((rows, rows), jnp.float32)],
        compiler_params=pltpu.CompilerParams(vmem_limit_bytes=60 * MIB),
        name="response",
    )(weight, half0, half1, green, part)


def chi_terms(tiles, blocks, col_counts, block_sizes, occ, weight, virt_green):
    devices = lax.axis_size("ten")
    aux_rows = blocks.shape[1]
    own = weight.shape[0]
    got = []
    for lo, hi in ((0, FIRST), (FIRST, tiles)):
        half = half_transform(blocks, col_counts, block_sizes, occ, lo, hi)
        half = half.reshape(devices, own, aux_rows, (hi - lo) * LANES)
        got.append(lax.all_to_all(half, "ten", split_axis=0, concat_axis=0, tiled=True))
    green = pack_green(block_sizes, virt_green, tiles * LANES)
    part = dress(got[0], green)
    return response(got[0], got[1], weight, part, green)


def per_device(blocks, col_counts, block_sizes, occ_coeff, occ_weight, virt_green):
    devices = lax.axis_size("ten")
    aux_rows = blocks.shape[1]
    own = occ_coeff.shape[1] // devices
    occ = occ_coeff.astype(jnp.float32)
    weight = lax.dynamic_slice(occ_weight, (lax.axis_index("ten") * own,), (own,))
    used = jnp.sum(block_sizes)
    case = sum((used > tiles * LANES).astype(jnp.int32) for tiles in WIDTHS[:-1])
    terms = lax.switch(
        case,
        [functools.partial(chi_terms, tiles) for tiles in WIDTHS],
        blocks, col_counts, block_sizes, occ, weight, virt_green,
    )
    terms = terms.reshape(devices, aux_rows, devices * aux_rows)
    terms = lax.all_to_all(terms, "ten", split_axis=0, concat_axis=0, tiled=True)
    share = jnp.sum(terms.astype(jnp.float32), axis=0)
    groups = lax.axis_size("rep")
    one, two, three = (
        lax.ppermute(share, "rep", [(z, (z + step) % groups) for z in range(groups)]) for step in (1, 2, 3)
    )
    return (share + two) + (one + three)


def solution(mesh):
    return jax.shard_map(
        per_device,
        mesh=mesh,
        in_specs=(P(None, "ten", None), P(), P(), P(None, "rep"), P("rep"), P()),
        out_specs=P("ten", None),
        check_vma=False,
    )
```

time: 122 us -> 116 us (0.951)
  waiting for transfers between devices: 37.9 us -> 12.7 us
  Pallas kernels: 43.5 us -> 60.2 us
  between operations: 0.06 us -> 1.98 us
  other arithmetic: 0.71 us -> 2.07 us
    all_to_all x2, waiting for transfers between devices: 34.9 us -> 9.68 us  [chi_terms(): lax.all_to_all(half, 'ten', split_axis=0, concat_axis=0, tiled=True)]
    pallas_call x4 -> x5, Pallas kernels: 43.5 us -> 60.2 us  [the longest x2 23.6 us: half_transform(): pl.pallas_call(functools.partial(half_kernel, lo, hi), out_shape=jax.Shap...]
    reshape x2 -> x0, local copies, waits for them, and re-layouts: 2.16 us -> none  [per_device(): occ_coeff.astype(jnp.float32).reshape(devices * BS // 2, 2 * occ_count)]
    cond x0 -> x8, local copies, waits for them, and re-layouts: none -> 1.39 us
    reduce_sum x0 -> x1, other arithmetic: none -> 1.29 us  [per_device(): used = jnp.sum(block_sizes)]
  transfers between devices with their start and end apart: 5 -> 5, of which waited for: 4 -> 4; matrix products, arithmetic and copies ran while one was open for 0% -> 0% of each run, Pallas kernels for 18% -> 33%
where the time goes in v2:
time: 116 us; the launch traced here: 115 us
  Pallas kernels  60.2 us (52%)
  starting transfers between devices  18.6 us (16%)
  blocking collectives  16.2 us (14%)
  waiting for transfers between devices  12.7 us (11%)
  local copies, waits for them, and re-layouts  3.35 us (3%)
  other arithmetic  2.07 us (2%)
  between operations  1.98 us (2%)
    pallas_call x2, Pallas kernels, half_transform(): pl.pallas_call(functools.partial(half_kernel, lo, hi), out_shape=jax.Shap...  23.6 us
    pallas_call x1, Pallas kernels, pack_green(): pl.pallas_call(pack_kernel, out_shape=jax.ShapeDtypeStruct((width, width)...  16.2 us
    all_to_all x1, blocking collectives, per_device(): lax.all_to_all(terms, 'ten', split_axis=0, concat_axis=0, tiled=True)  16.2 us
    all_to_all x2, starting transfers between devices, chi_terms(): lax.all_to_all(half, 'ten', split_axis=0, concat_axis=0, tiled=True)  13.5 us
    pallas_call x1, Pallas kernels, response(): pl.pallas_call(functools.partial(response_kernel, depth0, width), grid=(p...  12.7 us
    all_to_all x2, waiting for transfers between devices, chi_terms(): lax.all_to_all(half, 'ten', split_axis=0, concat_axis=0, tiled=True)  9.68 us
    pallas_call x1, Pallas kernels, dress(): pl.pallas_call(dress_kernel, grid=(steps,), out_shape=jax.ShapeDtypeStruc...  7.81 us
    ppermute x3, starting transfers between devices, per_device(): lax.ppermute(share, 'rep', [(z, (z + step) % groups) for z in range(group...  5.14 us
  transfers between devices with their start and end apart: 5, of which 4 were waited for; matrix products, arithmetic and copies ran while one was open for 0% of the time, Pallas kernels for 33%

profile of v2, /device:TPU:1, one launch (start us, length us, event | category | flops | bytes accessed | tf_op | source)
XLA Modules:
  0.0 115.2 jit_solution(3041569315375396854)
XLA Ops:
  0.0 1.3 %reduce_sum.18 = s32[]{:T(128)} reduce(s32[32]{0:T(128)} %param.12, s32[]{:T(128)} %constant.9.clone.1), dimensions={0}, to_apply=%region_0.0 | reduce | flops 31 | bytes 136 | tf_op jit(solution)/shard_map/reduce_sum | solution.py:402
  3.2 1.2 %copy.7 = bf16[2048,64]{1,0:T(8,128)(2,1)S(1)} copy(bf16[2048,64]{0,1:T(8,128)(2,1)} %param.13) | data formatting | bytes 524288 | tf_op args[3]
  4.5 0.1 convert_element_type.18
  4.6 0.7 dynamic_slice.3
  5.3 84.8 %conditional.1 = (bf16[512,512]{1,0:T(8,128)(2,1)}) conditional(s32[]{:T(128)} %clamp.3, (s32[32]{0:T(128)}, s32[32]{0:T(128)}, f32[2048,64]{1,0:T(8,128)S(1)}, bf16[64,16,4096]{2,1,0:T(8,128)(2,1)}, bf16[2048,2048]{1,0:T(8,128)(2,1)}, /*index=5*/f32[2]{0:T(128)S(1)}) %tuple.17, (s32[32]{0:T(128)}, s32[32]{0:T(128)}, ...), branch_computations={%region_1.0_spmd, %region_2.0_spmd, %region_3.0_spmd, %region_4.0_... | conditional | flops 28147482624 | bytes 72352952 | solution.py:404
  5.3 0.0 copy-start.9
  5.3 0.0 copy-start.13
  5.3 9.2 %half_transform.10 = bf16[1024,512]{1,0:T(8,128)(2,1)} custom-call(s32[32]{0:T(128)} %get-tuple-element.65.counts_ref, s32[32]{0:T(128)} %get-tuple-element.66.sizes_ref, f32[2048,64]{1,0:T(8,128)S(1)} %get-tuple-element.67.occ_ref, bf16[64,16,4096]{2,1,0:T(8,128)(2,1)} %get-tuple-element.68.blocks_ref), custom_call_target="tpu_custom_call" | custom-call | flops 4000000000 | bytes 4194304 | tf_op jit(solution)/shard_map/cond/branch_1_fun/half_transform/pallas_call | solution.py:175
  14.5 8.6 %all-to-all-start.2 = ((bf16[32,2,16,512]{3,2,1,0:T(8,128)(2,1)}), bf16[32,2,16,512]{3,2,1,0:T(8,128)(2,1)S(1)}, u32[]{:S(2)}, u32[]{:S(2)}) async-start(bf16[32,2,16,512]{3,2,1,0:T(8,128)(2,1)} %bitcast.14), calls=%async_computation.2 | async-start | bytes 2097152 | tf_op jit(solution)/shard_map/cond/branch_1_fun/all_to_all | solution.py:390
  23.1 0.0 copy-done.9
  23.1 0.0 copy-done.13
  23.2 14.3 %half_transform.11 = bf16[1024,1152]{1,0:T(8,128)(2,1)} custom-call(s32[32]{0:T(128)S(1)} %copy-done.13, s32[32]{0:T(128)S(1)} %copy-done.9, f32[2048,64]{1,0:T(8,128)S(1)} %get-tuple-element.67.occ_ref, bf16[64,16,4096]{2,1,0:T(8,128)(2,1)} %get-tuple-element.68.blocks_ref), custom_call_target="tpu_custom_call" | custom-call | flops 8999999488 | bytes 9437184 | tf_op jit(solution)/shard_map/cond/branch_1_fun/half_transform/pallas_call | solution.py:175
  37.5 2.6 %all-to-all-done.2.half_ref.half0_ref = bf16[32,2,16,512]{3,2,1,0:T(8,128)(2,1)S(1)} async-done(((bf16[32,2,16,512]{3,2,1,0:T(8,128)(2,1)}), bf16[32,2,16,512]{3,2,1,0:T(8,128)(2,1)S(1)}, u32[]{:S(2)}, u32[]{:S(2)}) %all-to-all-start.2) | async-done | bytes 1048608 | tf_op jit(solution)/shard_map/cond/branch_1_fun/all_to_all | solution.py:390
  40.0 0.0 copy-start.6
  40.1 4.9 %all-to-all-start.3 = ((bf16[32,2,16,1152]{3,2,1,0:T(8,128)(2,1)}), bf16[32,2,16,1152]{3,2,1,0:T(8,128)(2,1)S(1)}, u32[]{:S(2)}, u32[]{:S(2)}) async-start(bf16[32,2,16,1152]{3,2,1,0:T(8,128)(2,1)} %bitcast.11), calls=%async_computation.3 | async-start | bytes 4718592 | tf_op jit(solution)/shard_map/cond/branch_1_fun/all_to_all | solution.py:390
  44.9 16.2 %pack_green.5.green_ref = bf16[1664,1664]{1,0:T(8,128)(2,1)} custom-call(s32[32]{0:T(128)S(1)} %copy-done.9, bf16[2048,2048]{1,0:T(8,128)(2,1)} %get-tuple-element.69.green_ref), custom_call_target="tpu_custom_call" | custom-call | flops 10000000000 | bytes 14680064 | tf_op jit(solution)/shard_map/cond/branch_1_fun/pack_green/pallas_call | solution.py:267
  61.1 0.0 copy-done.6
  61.1 7.8 %dress.5.part_ref = f32[2,512,1792]{2,1,0:T(8,128)} custom-call(bf16[32,2,16,512]{3,2,1,0:T(8,128)(2,1)} %copy-done.6, bf16[1664,1664]{1,0:T(8,128)(2,1)} %pack_green.5.green_ref), custom_call_target="tpu_custom_call" | custom-call | flops 1744830464 | bytes 9568256 | tf_op jit(solution)/shard_map/cond/branch_1_fun/dress/pallas_call | solution.py:302
  68.9 7.1 %all-to-all-done.3.half1_ref = bf16[32,2,16,1152]{3,2,1,0:T(8,128)(2,1)S(1)} async-done(((bf16[32,2,16,1152]{3,2,1,0:T(8,128)(2,1)}), bf16[32,2,16,1152]{3,2,1,0:T(8,128)(2,1)S(1)}, u32[]{:S(2)}, u32[]{:S(2)}) %all-to-all-start.3) | async-done | bytes 2359328 | tf_op jit(solution)/shard_map/cond/branch_1_fun/all_to_all | solution.py:390
  76.1 0.0 copy-start.2
  76.1 1.4 %copy-done.2 = bf16[32,2,16,1152]{3,2,1,0:T(8,128)(2,1)} copy-done((bf16[32,2,16,1152]{3,2,1,0:T(8,128)(2,1)}, bf16[32,2,16,1152]{3,2,1,0:T(8,128)(2,1)S(1)}, u32[]{:S(2)}) %copy-start.2) | copy-done | bytes 2359320 | tf_op jit(solution)/shard_map/cond
  77.4 12.7 %response.5 = bf16[512,512]{1,0:T(8,128)(2,1)} custom-call(f32[2]{0:T(128)S(1)} %get-tuple-element.64.weight_ref, bf16[32,2,16,512]{3,2,1,0:T(8,128)(2,1)} %copy-done.6, bf16[32,2,16,1152]{3,2,1,0:T(8,128)(2,1)} %copy-done.2, bf16[1664,1664]{1,0:T(8,128)(2,1)} %pack_green.5.green_ref, f32[2,512,1792]{2,1,0:T(8,128)} %dress.5.part_ref), custom_call_target="tpu_custom_call" | custom-call | tf_op jit(solution)/shard_map/cond/branch_1_fun/response/pallas_call | solution.py:364
  90.1 16.2 %all_to_all.37 = bf16[32,16,512]{2,1,0:T(8,128)(2,1)S(1)} all-to-all(bf16[32,16,512]{2,1,0:T(8,128)(2,1)} %bitcast.8), channel_id=1, replica_groups=mesh['rep'=4,'ten'=32] {'ten'}, dimensions={0} | all-to-all | bytes 1048576 | tf_op jit(solution)/shard_map/all_to_all | solution.py:410
  106.3 0.1 convert_reduce_fusion
  106.3 3.8 %collective-permute-start.2 = (f32[16,512]{1,0:T(8,128)S(1)}, f32[16,512]{1,0:T(8,128)S(1)}, u32[]{:S(2)}, u32[]{:S(2)}) collective-permute-start(f32[16,512]{1,0:T(8,128)S(1)} %convert_reduce_fusion), channel_id=1, source_target_pairs={{0,96},{32,0},{64,32},{96,64},{1,97},{33,1},{65,33},{97,65},{2,98}... | collective-permute-start | bytes 98312 | tf_op jit(solution)/shard_map/ppermute | solution.py:414
  110.2 0.0 collective-permute-start.1
  110.2 1.3 %collective-permute-start = (f32[16,512]{1,0:T(8,128)S(1)}, f32[16,512]{1,0:T(8,128)S(1)}, u32[]{:S(2)}, u32[]{:S(2)}) collective-permute-start(f32[16,512]{1,0:T(8,128)S(1)} %convert_reduce_fusion), channel_id=1, source_target_pairs={{0,64},{32,96},{64,0},{96,32},{1,65},{33,97},{65,1},{97,33},{2,66}... | collective-permute-start | bytes 98312 | tf_op jit(solution)/shard_map/ppermute | solution.py:414
  111.5 0.0 collective-permute-done.2
  111.5 2.7 %collective-permute-done.1 = f32[16,512]{1,0:T(8,128)S(1)} collective-permute-done((f32[16,512]{1,0:T(8,128)S(1)}, f32[16,512]{1,0:T(8,128)S(1)}, u32[]{:S(2)}, u32[]{:S(2)}) %collective-permute-start.1) | collective-permute-done | bytes 32800 | tf_op jit(solution)/shard_map/ppermute | solution.py:414
  114.2 0.4 collective-permute-done
  114.5 0.6 add_add_fusion
Async XLA Ops:
  5.3 17.8 %copy-start.9 = (s32[32]{0:T(128)S(1)}, s32[32]{0:T(128)}, u32[]{:S(2)}) copy-start(s32[32]{0:T(128)} %get-tuple-element.66.sizes_ref) | copy-start | bytes 388 | tf_op jit(solution)/shard_map/cond
  5.3 17.9 %copy-start.13 = (s32[32]{0:T(128)S(1)}, s32[32]{0:T(128)}, u32[]{:S(2)}) copy-start(s32[32]{0:T(128)} %get-tuple-element.65.counts_ref) | copy-start | bytes 388 | tf_op jit(solution)/shard_map/cond
  14.5 25.5 %all-to-all-start.2 = ((bf16[32,2,16,512]{3,2,1,0:T(8,128)(2,1)}), bf16[32,2,16,512]{3,2,1,0:T(8,128)(2,1)S(1)}, u32[]{:S(2)}, u32[]{:S(2)}) async-start(bf16[32,2,16,512]{3,2,1,0:T(8,128)(2,1)} %bitcast.14), calls=%async_computation.2 | async-start | bytes 2097152 | tf_op jit(solution)/shard_map/cond/branch_1_fun/all_to_all | solution.py:390
  40.0 21.1 %copy-start.6 = (bf16[32,2,16,512]{3,2,1,0:T(8,128)(2,1)}, bf16[32,2,16,512]{3,2,1,0:T(8,128)(2,1)S(1)}, u32[]{:S(2)}) copy-start(bf16[32,2,16,512]{3,2,1,0:T(8,128)(2,1)S(1)} %all-to-all-done.2.half_ref.half0_ref) | copy-start | bytes 3145732 | tf_op jit(solution)/shard_map/cond
  40.1 36.0 %all-to-all-start.3 = ((bf16[32,2,16,1152]{3,2,1,0:T(8,128)(2,1)}), bf16[32,2,16,1152]{3,2,1,0:T(8,128)(2,1)S(1)}, u32[]{:S(2)}, u32[]{:S(2)}) async-start(bf16[32,2,16,1152]{3,2,1,0:T(8,128)(2,1)} %bitcast.11), calls=%async_computation.3 | async-start | bytes 4718592 | tf_op jit(solution)/shard_map/cond/branch_1_fun/all_to_all | solution.py:390
  76.1 1.4 %copy-start.2 = (bf16[32,2,16,1152]{3,2,1,0:T(8,128)(2,1)}, bf16[32,2,16,1152]{3,2,1,0:T(8,128)(2,1)S(1)}, u32[]{:S(2)}) copy-start(bf16[32,2,16,1152]{3,2,1,0:T(8,128)(2,1)S(1)} %all-to-all-done.3.half1_ref) | copy-start | bytes 7077892 | tf_op jit(solution)/shard_map/cond
  106.3 5.1 %collective-permute-start.2 = (f32[16,512]{1,0:T(8,128)S(1)}, f32[16,512]{1,0:T(8,128)S(1)}, u32[]{:S(2)}, u32[]{:S(2)}) collective-permute-start(f32[16,512]{1,0:T(8,128)S(1)} %convert_reduce_fusion), channel_id=1, source_target_pairs={{0,96},{32,0},{64,32},{96,64},{1,97},{33,1},{65,33},{97,65},{2,98}... | collective-permute-start | bytes 98312 | tf_op jit(solution)/shard_map/ppermute | solution.py:414
  110.2 4.0 %collective-permute-start.1 = (f32[16,512]{1,0:T(8,128)S(1)}, f32[16,512]{1,0:T(8,128)S(1)}, u32[]{:S(2)}, u32[]{:S(2)}) collective-permute-start(f32[16,512]{1,0:T(8,128)S(1)} %convert_reduce_fusion), channel_id=1, source_target_pairs={{0,32},{32,64},{64,96},{96,0},{1,33},{33,65},{65,97},{97,1},{2,34}... | collective-permute-start | bytes 98312 | tf_op jit(solution)/shard_map/ppermute | solution.py:414
  110.2 4.4 %collective-permute-start = (f32[16,512]{1,0:T(8,128)S(1)}, f32[16,512]{1,0:T(8,128)S(1)}, u32[]{:S(2)}, u32[]{:S(2)}) collective-permute-start(f32[16,512]{1,0:T(8,128)S(1)} %convert_reduce_fusion), channel_id=1, source_target_pairs={{0,64},{32,96},{64,0},{96,32},{1,65},{33,97},{65,1},{97,33},{2,66}... | collective-permute-start | bytes 98312 | tf_op jit(solution)/shard_map/ppermute | solution.py:414
